TPU v7x, 256 devices: a whole 4x4x8 slice. The times are simulated.
256 devices in a mesh: blk: 32 (over y_lo, z, core), dp: 8 (over x, y_hi).
Axes of the slice: x: 4, y: 4 (y_hi: 2, y_lo: 2; y = y_hi * 2 + y_lo), z: 8, core: 2. Of those that a mesh axis runs over, the one named last changes fastest.
Arguments:
- residuals: bfloat16 [32768, 768], P(('blk', 'dp')), may hold values from -130 to 130
- codebook: bfloat16 [24576, 768], P('blk'), may hold values from -9 to 9
- section_codes: int32 [32768], P(('blk', 'dp')), may hold values from 0 to 1023, as said below
- code_owner: int32 [1024], replicated, may hold values from 0 to 31, as said below
Outputs:
- new_codebook: float32 [24576, 768], P('blk')
- code_shift: float32 [2048, 768], P('blk')
Inputs may be any that keep to these rules, and one draw needn't show every extreme that they name: `section_codes`: among the rows of one device, at most 12 have section-one codes owned by one codeword block, and in every device's rows some block is named exactly 12 times. `code_owner`: each codeword block owns at least one and at most 64 section-one codes; some block owns exactly 64.
All inputs are finite; a program needn't handle non-finite values.
Results may differ from a plain program's by a relative error of at most 0.002.
Values may be sent and summed in bfloat16 or wider, within the bound.
No kernel may reach another device: no remote copies, remote signals or barrier semaphores. Data moves between devices by JAX's collectives and lax.ppermute only.
A program may use at most 128 MiB of HBM per device.

v0:
```python
import math
import jax
import jax.numpy as jnp
from jax import lax
from jax.sharding import PartitionSpec as P

SLOTS = 64
prior_weight = 0.5


def merged(value, axis, join):
    pieces = jax.tree.map(lambda part: lax.all_gather(part, axis), value)
    head = jax.tree.map(lambda part: part[0], pieces)
    tail = jax.tree.map(lambda part: part[1:], pieces)
    running, _ = lax.scan(lambda running, section: (join(running, section), None), head, tail)
    return running


def score_block(rows, codebook, half_norm):
    raw = lax.dot_general(
        rows, codebook, (((1,), (1,)), ((), ())), preferred_element_type=jnp.float32
    )
    return (raw - half_norm[None, :]) * (2.0 / math.sqrt(rows.shape[1]))


def block_rows():
    return 512


def row_stats(rows, codebook, half_norm):
    count = rows.shape[0]
    size = block_rows()
    stacked = rows.reshape(count // size, size, rows.shape[1])

    def one_block(block):
        scores = score_block(block, codebook, half_norm)
        top = jnp.max(scores, axis=1)
        total = jnp.sum(jnp.exp(scores - top[:, None]), axis=1)
        return (top, total)

    top, total = lax.map(one_block, stacked)
    return (top.reshape(-1), total.reshape(-1))


def accumulate(carry, rows, top, total, codebook, half_norm):
    count = rows.shape[0]
    size = block_rows()
    stacked = rows.reshape(count // size, size, rows.shape[1])
    tops = top.reshape(count // size, size)
    totals = total.reshape(count // size, size)

    def add_weights(state, block, scores, block_top, block_total):
        weights = (jnp.exp(scores - block_top[:, None]) / block_total[:, None]).astype(jnp.bfloat16)
        weighted = state[0] + lax.dot_general(
            weights, block, (((0,), (0,)), ((), ())), preferred_element_type=jnp.float32
        )
        mass = state[1] + jnp.sum(weights.astype(jnp.float32), axis=0)
        return (weighted, mass)

    def fresh_block(state, item):
        block, block_top, block_total = item
        scores = score_block(block, codebook, half_norm)
        return (add_weights(state, block, scores, block_top, block_total), None)

    result, _ = lax.scan(fresh_block, carry, (stacked, tops, totals))
    return result


def combine_stats(first, second):
    top = jnp.maximum(first[0], second[0])
    total = first[1] * jnp.exp(first[0] - top) + second[1] * jnp.exp(second[0] - top)
    return (top, total)


def local(residuals, codebook, section_codes, code_owner):
    nblk = lax.axis_size("blk")
    row_count, width = residuals.shape
    half_norm = 0.5 * jnp.sum(jnp.square(codebook.astype(jnp.float32)), axis=1)
    top, total = row_stats(
        lax.all_gather(residuals, "blk", axis=0, tiled=True), codebook, half_norm
    )
    local_stats = (top, total)
    top_all, total_all = merged(local_stats, "blk", combine_stats)
    zero_sums = (
        jnp.zeros((codebook.shape[0], width), jnp.float32),
        jnp.zeros((codebook.shape[0],), jnp.float32),
    )
    top = top_all
    total = total_all
    weighted, mass = accumulate(
        zero_sums,
        lax.all_gather(residuals, "blk", axis=0, tiled=True),
        top,
        total,
        codebook,
        half_norm,
    )
    code_count = code_owner.shape[0]
    owner_hot = (code_owner[:, None] == jnp.arange(nblk, dtype=jnp.int32)[None, :]).astype(
        jnp.int32
    )
    before = jnp.cumsum(owner_hot, axis=0) - owner_hot
    rank = jnp.sum(before * owner_hot, axis=1)
    code_slot = code_owner * SLOTS + rank
    code_hit = section_codes[:, None] == jnp.arange(code_count, dtype=jnp.int32)[None, :]
    row_slot = jnp.sum(jnp.where(code_hit, code_slot[None, :], 0), axis=1)
    capacity = max(2, 3 * row_count // nblk)
    target = row_slot // SLOTS
    local_slot = row_slot - target * SLOTS
    target_hot = (target[:, None] == jnp.arange(nblk, dtype=jnp.int32)[None, :]).astype(jnp.int32)
    earlier = jnp.cumsum(target_hot, axis=0) - target_hot
    position = jnp.sum(earlier * target_hot, axis=1)
    flat_index = target * capacity + position
    row_buffer = jnp.zeros((nblk * capacity, width), jnp.bfloat16).at[flat_index].set(residuals)
    slot_hot = (local_slot[:, None] == jnp.arange(SLOTS, dtype=jnp.int32)[None, :]).astype(
        jnp.bfloat16
    )
    tag_buffer = jnp.zeros((nblk * capacity, SLOTS), jnp.bfloat16).at[flat_index].set(slot_hot)
    got_rows, got_tags = (
        lax.all_to_all(
            row_buffer.reshape(nblk, capacity, width),
            "blk",
            split_axis=0,
            concat_axis=0,
            tiled=True,
        ),
        lax.all_to_all(
            tag_buffer.reshape(nblk, capacity, SLOTS),
            "blk",
            split_axis=0,
            concat_axis=0,
            tiled=True,
        ),
    )
    tags_flat = got_tags.reshape(nblk * capacity, SLOTS)
    shift_sum = lax.dot_general(
        tags_flat,
        got_rows.reshape(nblk * capacity, width),
        (((0,), (0,)), ((), ())),
        preferred_element_type=jnp.float32,
    )
    shift_count = jnp.sum(tags_flat.astype(jnp.float32), axis=0)
    weighted, mass, shift_sum, shift_count = lax.psum(
        (weighted, mass, shift_sum, shift_count), "dp"
    )
    new_codebook = (weighted + prior_weight * codebook.astype(jnp.float32)) / (mass + prior_weight)[
        :, None
    ]
    code_shift = shift_sum / (shift_count + 1.0)[:, None]
    return (new_codebook, code_shift)


def solution(mesh):
    in_specs = (P(("blk", "dp"), None), P("blk", None), P(("blk", "dp")), P())
    out_specs = (P("blk", None), P("blk", None))
    return jax.shard_map(local, mesh=mesh, in_specs=in_specs, out_specs=out_specs, check_vma=False)
```

profile of v0, /device:TPU:50, one launch (start us, length us, event | category | flops | bytes accessed | tf_op | source)
XLA Modules:
  0.0 416.6 jit_solution(8335260162383934717)
XLA Ops:
  8.6 9.0 %reduce-window.6 = s32[32,8,128]{2,1,0:T(8,128)S(1)} reduce-window(s32[32,8,128]{2,1,0:T(8,128)S(1)} %fusion.18, s32[]{:T(128)} %constant.71.clone.1), window={size=1x1x128 pad=0_0x0_0x127_0}, to_apply=%region_12.13 | reduce-window | flops 4161536 | bytes 262148 | tf_op jit(solution)/shard_map/reduce-window
  22.6 9.4 %all-to-all-start = ((bf16[32,2,384]{2,1,0:T(2,128)(2,1)}), bf16[32,2,384]{2,1,0:T(2,128)(2,1)S(1)}, u32[]{:S(2)}, u32[]{:S(2)}) async-start(bf16[32,2,384]{2,1,0:T(2,128)(2,1)} %reshape.162), calls=%async_computation | async-start | bytes 98304 | tf_op jit(solution)/shard_map/all_to_all | solution.py:127
  32.1 1.7 scatter_custom_fusion.1
  34.8 5.1 %all-to-all-done = bf16[32,2,384]{2,1,0:T(2,128)(2,1)S(1)} async-done(((bf16[32,2,384]{2,1,0:T(2,128)(2,1)}), bf16[32,2,384]{2,1,0:T(2,128)(2,1)S(1)}, u32[]{:S(2)}, u32[]{:S(2)}) %all-to-all-start) | async-done | bytes 49184 | tf_op jit(solution)/shard_map/all_to_all | solution.py:127
  39.9 5.0 %all-to-all-start.1 = ((bf16[32,12,768]{2,1,0:T(8,128)(2,1)}), bf16[32,12,768]{2,1,0:T(8,128)(2,1)S(1)}, u32[]{:S(2)}, u32[]{:S(2)}) async-start(bf16[32,12,768]{2,1,0:T(8,128)(2,1)} %reshape.128), calls=%async_computation.1 | async-start | bytes 1572864 | tf_op jit(solution)/shard_map/all_to_all | solution.py:120
  45.0 1.6 fusion.9
  46.8 30.1 %all-to-all-done.1 = bf16[32,12,768]{2,1,0:T(8,128)(2,1)S(1)} async-done(((bf16[32,12,768]{2,1,0:T(8,128)(2,1)}), bf16[32,12,768]{2,1,0:T(8,128)(2,1)S(1)}, u32[]{:S(2)}, u32[]{:S(2)}) %all-to-all-start.1) | async-done | bytes 589856 | tf_op jit(solution)/shard_map/all_to_all | solution.py:120
  77.9 16.4 %all-gather.4.cloned.1.call-done = bf16[4096,768]{1,0:T(8,128)(2,1)} async-done(((bf16[128,768]{1,0:T(8,128)(2,1)}), bf16[4096,768]{1,0:T(8,128)(2,1)}) %all-gather.4.cloned.1.call-update) | async-done | bytes 6291472 | tf_op jit(solution)/shard_map/all_gather | solution.py:92
  94.3 33.8 %while.37 = (s32[]{:T(128)}, f32[8,512]{1,0:T(8,128)S(1)}, f32[8,512]{1,0:T(8,128)}, bf16[8,512,768]{2,1,0:T(8,128)(2,1)}, bf16[768,768]{1,0:T(8,128)(2,1)}, /*index=5*/f32[768]{0:T(1024)S(1)}, s32[]{:T(128)}, s32[]{:T(128)}) while((s32[]{:T(128)}, f32[8,512]{1,0:T(8,128)S(1)}, f32[8,512]{1,0:T(8,128)}, bf16[8,512,768]{2,1,0:T(8,128)(2,1)}, ...), condition=%wide.region_4.5_spmd, body=%wide.region_1.4_spmd.sunk | while | flops 605944832 | bytes 5129821 | solution.py:41
  94.3 2.4 fusion.37
  97.2 1.3 dynamic_update_slice.10
  98.5 2.4 fusion.37
  101.4 1.3 dynamic_update_slice.10
  102.8 2.4 fusion.37
  105.6 1.3 dynamic_update_slice.10
  107.0 2.4 fusion.37
  109.8 1.3 dynamic_update_slice.10
  111.2 2.4 fusion.37
  114.1 1.3 dynamic_update_slice.10
  115.5 2.4 fusion.37
  118.3 1.3 dynamic_update_slice.10
  119.7 2.4 fusion.37
  123.9 2.4 fusion.37
  128.7 33.0 %all-gather = f32[32,1,4096]{2,1,0:T(1,128)S(1)} all-gather(f32[1,1,4096]{2,1,0:T(1,128)S(1)} %reshape.145), channel_id=1, replica_groups=mesh['blk'=32,'dp'=8] {'blk'}, dimensions={0}, use_global_device_ids=true | all-gather | bytes 540672 | tf_op jit(solution)/shard_map/all_gather | solution.py:12
  161.8 34.3 %all-gather.1 = f32[32,1,4096]{2,1,0:T(1,128)S(1)} all-gather(f32[1,1,4096]{2,1,0:T(1,128)S(1)} %reshape.147), channel_id=1, replica_groups=mesh['blk'=32,'dp'=8] {'blk'}, dimensions={0}, use_global_device_ids=true | all-gather | bytes 540672 | tf_op jit(solution)/shard_map/all_gather | solution.py:12
  197.5 30.3 %while.38 = (s32[]{:T(128)}, f32[4096]{0:T(1024)S(1)}, f32[4096]{0:T(1024)S(1)}, f32[31,4096]{1,0:T(8,128)}, f32[31,4096]{1,0:T(8,128)S(1)}, /*index=5*/s32[]{:T(128)}) while((s32[]{:T(128)}, f32[4096]{0:T(1024)S(1)}, f32[4096]{0:T(1024)S(1)}, f32[31,4096]{1,0:T(8,128)}, f32[31,4096]{1,0:T(8,128)S(1)}, /*index=5*/s32[]{:T(128)}) %tuple.87), condition=%wide.region_6.7_spmd, body=%wide.region_5.6_spmd.sunk | while | flops 24578 | bytes 163913 | solution.py:15
  227.8 44.6 %while.39 = (s32[]{:T(128)}, f32[768,768]{1,0:T(8,128)S(1)}, f32[768]{0:T(1024)}, bf16[8,512,768]{2,1,0:T(8,128)(2,1)}, bf16[768,768]{1,0:T(8,128)(2,1)}, /*inde...) while((s32[]{:T(128)}, f32[768,768]{1,0:T(8,128)S(1)}, ...), condition=%wide.region_9.10_spmd.clone, body=%wide.region_7.9_spmd.clone.sunk | while | flops 1211892480 | bytes 9098412 | solution.py:65
  227.8 2.4 convert_reduce_fusion.3
  230.3 2.5 select_add_fusion.4
  233.4 2.4 convert_reduce_fusion.3
  235.9 2.5 select_add_fusion.4
  239.0 2.4 convert_reduce_fusion.3
  241.4 2.5 select_add_fusion.4
  244.6 2.4 convert_reduce_fusion.3
  247.0 2.5 select_add_fusion.4
  250.1 2.4 convert_reduce_fusion.3
  252.6 2.5 select_add_fusion.4
  255.7 2.4 convert_reduce_fusion.3
  258.2 2.5 select_add_fusion.4
  261.3 2.4 convert_reduce_fusion.3
  263.7 2.5 select_add_fusion.4
  266.9 2.4 convert_reduce_fusion.3
  269.3 2.5 select_add_fusion.4
  272.4 1.4 copy-done
  273.9 23.1 %all-reduce = (f32[768]{0:T(1024)S(1)}, f32[64]{0:T(128)S(1)}) all-reduce(f32[768]{0:T(1024)S(1)} %copy-done.3, f32[64]{0:T(128)S(1)} %convert_reduce_fusion.1), channel_id=1, replica_groups=mesh['blk'=32,'dp'=8] {'dp'}, use_global_device_ids=true, to_apply=%region_11.12 | all-reduce | flops 832 | bytes 6656 | tf_op jit(solution)/shard_map/psum | solution.py:143
  297.1 107.2 %all-reduce.4.cloned.1.call-done = (f32[768,768]{1,0:T(8,128)}, f32[64,768]{1,0:T(8,128)}) async-done(((f32[768,768]{1,0:T(8,128)}, f32[64,768]{1,0:T(8,128)}), (f32[768,768]{1,0:T(8,128)}, f32[64,768]{1,0:T(8,128)})) %all-reduce.4.cloned.1.call-update) | async-done | bytes 2555920 | tf_op jit(solution)/shard_map/psum | solution.py:143
  404.3 1.7 broadcast_divide_fusion
  406.0 3.7 fusion.11
  (178 shorter events, 51.4 us)
Async XLA Ops:
  7.2 87.2 %all-gather.4.cloned.1.call-start = ((), (), s32[]{:S(2)}) async-start(), calls=%async_computation.2 | async-start | bytes 6488064 | tf_op jit(solution)/shard_map/all_gather | solution.py:92
  22.6 17.3 %all-to-all-start = ((bf16[32,2,384]{2,1,0:T(2,128)(2,1)}), bf16[32,2,384]{2,1,0:T(2,128)(2,1)S(1)}, u32[]{:S(2)}, u32[]{:S(2)}) async-start(bf16[32,2,384]{2,1,0:T(2,128)(2,1)} %reshape.162), calls=%async_computation | async-start | bytes 98304 | tf_op jit(solution)/shard_map/all_to_all | solution.py:127
  39.9 36.9 %all-to-all-start.1 = ((bf16[32,12,768]{2,1,0:T(8,128)(2,1)}), bf16[32,12,768]{2,1,0:T(8,128)(2,1)S(1)}, u32[]{:S(2)}, u32[]{:S(2)}) async-start(bf16[32,12,768]{2,1,0:T(8,128)(2,1)} %reshape.128), calls=%async_computation.1 | async-start | bytes 1572864 | tf_op jit(solution)/shard_map/all_to_all | solution.py:120
  45.0 359.4 %all-reduce.4.cloned.1.call-start = ((), (), s32[]{:S(2)}) async-start(), calls=%async_computation.3 | async-start | bytes 5111808 | tf_op jit(solution)/shard_map/psum | solution.py:143
  128.1 0.6 copy-start.5
  128.1 33.6 %copy-start.4 = (f32[8,512]{1,0:T(8,128)S(1)}, f32[8,512]{1,0:T(8,128)}, u32[]{:S(2)}) copy-start(f32[8,512]{1,0:T(8,128)} %get-tuple-element.107) | copy-start | bytes 49156
  230.3 2.5 copy-start.1
  232.8 0.6 copy-start.2
  235.9 2.5 copy-start.1
  238.4 0.6 copy-start.2
  241.4 2.5 copy-start.1
  244.0 0.6 copy-start.2
  247.0 2.5 copy-start.1
  249.5 0.6 copy-start.2
  252.6 2.5 copy-start.1
  255.1 0.6 copy-start.2
  258.2 2.5 copy-start.1
  260.7 0.6 copy-start.2
  263.7 2.5 copy-start.1
  266.3 0.6 copy-start.2
  269.3 2.5 copy-start.1
  271.8 0.6 copy-start.2
  272.4 1.4 copy-start
  272.4 1.5 copy-start.3
Sparse Core Ops, SparseCore 0:
  9.9 84.4 all-gather.3
  274.0 130.2 all-reduce.3
where the time goes:
time: 419 us; the launch traced here: 417 us
  waiting for transfers between devices  160 us (38%)
  blocking collectives  90.3 us (22%)
  matrix products  59.7 us (14%)
  local copies, waits for them, and re-layouts  52 us (12%)
  other arithmetic  24.8 us (6%)
  starting transfers between devices  14.5 us (3%)
  between operations  14.3 us (3%)
    psum x1, waiting for transfers between devices, local(): lax.psum((weighted, mass, shift_sum, shift_count), 'dp')  107 us
    all_gather x2, blocking collectives, merged(): pieces = jax.tree.map(lambda part: lax.all_gather(part, axis), value)  67.2 us
    dot_general x16, matrix products, score_block(): lax.dot_general(rows, codebook, (((1,), (1,)), ((), ())), preferred_eleme...  38.8 us
    all_to_all x1, waiting for transfers between devices, local(): lax.all_to_all(row_buffer.reshape(nblk, capacity, width), 'blk', split_ax...  30.1 us
    dynamic_slice x31, local copies, waits for them, and re-layouts, merged(): lax.scan(lambda running, section: (join(running, section), None), head, t...  28.9 us
    psum x1, blocking collectives, local(): lax.psum((weighted, mass, shift_sum, shift_count), 'dp')  23.1 us
    dot_general x8, matrix products, add_weights(): lax.dot_general(weights, block, (((0,), (0,)), ((), ())), preferred_eleme...  19.9 us
    all_gather x1, waiting for transfers between devices, local(): lax.all_gather(residuals, 'blk', axis=0, tiled=True)  16.4 us
  transfers between devices with their start and end apart: 4, of which 4 were waited for; matrix products, arithmetic and copies ran while one was open for 5% of the time, Pallas kernels for 0%

commit v1 on v0

--- a/solution.py
+++ b/solution.py
@@ -89,7 +89,9 @@
     total = total_all
     weighted, mass = accumulate(
         zero_sums,
-        lax.all_gather(residuals, "blk", axis=0, tiled=True),
+        jnp.concatenate(
+            lax.all_to_all(jnp.stack([residuals] * lax.axis_size("blk")), "blk", 0, 0), axis=0
+        ),
         top,
         total,
         codebook,

time: 419 us -> 510 us (1.22)
  blocking collectives: 90.3 us -> 164 us
  waiting for transfers between devices: 160 us -> 169 us
    all_gather x2, blocking collectives: 67.2 us -> 140 us  [merged(): pieces = jax.tree.map(lambda part: lax.all_gather(part, axis), value)]
    all_gather x1, waiting for transfers between devices: 16.4 us -> 25.1 us  [local(): lax.all_gather(residuals, 'blk', axis=0, tiled=True)]
  transfers between devices with their start and end apart: 4 -> 5, of which waited for: 4 -> 4; matrix products, arithmetic and copies ran while one was open for 5% -> 18% of each run, Pallas kernels for 0% -> 0%
where the time goes in v1:
time: 510 us; the launch traced here: 508 us
  waiting for transfers between devices  169 us (33%)
  blocking collectives  164 us (32%)
  matrix products  59.7 us (12%)
  local copies, waits for them, and re-layouts  56.2 us (11%)
  other arithmetic  24.8 us (5%)
  starting transfers between devices  19.2 us (4%)
  between operations  14.3 us (3%)
    all_gather x2, blocking collectives, merged(): pieces = jax.tree.map(lambda part: lax.all_gather(part, axis), value)  140 us
    psum x1, waiting for transfers between devices, local(): lax.psum((weighted, mass, shift_sum, shift_count), 'dp')  108 us
    dot_general x16, matrix products, score_block(): lax.dot_general(rows, codebook, (((1,), (1,)), ((), ())), preferred_eleme...  38.8 us
    all_to_all x1, waiting for transfers between devices, local(): lax.all_to_all(row_buffer.reshape(nblk, capacity, width), 'blk', split_ax...  30.2 us
    dynamic_slice x31, local copies, waits for them, and re-layouts, merged(): lax.scan(lambda running, section: (join(running, section), None), head, t...  28.9 us
    all_gather x1, waiting for transfers between devices, local(): lax.all_gather(residuals, 'blk', axis=0, tiled=True)  25.1 us
    psum x1, blocking collectives, local(): lax.psum((weighted, mass, shift_sum, shift_count), 'dp')  23.3 us
    dot_general x8, matrix products, add_weights(): lax.dot_general(weights, block, (((0,), (0,)), ((), ())), preferred_eleme...  19.9 us
  transfers between devices with their start and end apart: 5, of which 4 were waited for; matrix products, arithmetic and copies ran while one was open for 18% of the time, Pallas kernels for 0%

profile of v1, /device:TPU:50, one launch (start us, length us, event | category | flops | bytes accessed | tf_op | source)
XLA Modules:
  0.0 508.0 jit_solution(12497724867154783689)
XLA Ops:
  8.6 9.0 %reduce-window.6 = s32[32,8,128]{2,1,0:T(8,128)S(1)} reduce-window(s32[32,8,128]{2,1,0:T(8,128)S(1)} %fusion.18, s32[]{:T(128)} %constant.71.clone.1), window={size=1x1x128 pad=0_0x0_0x127_0}, to_apply=%region_12.13 | reduce-window | flops 4161536 | bytes 262148 | tf_op jit(solution)/shard_map/reduce-window
  22.6 9.4 %all-to-all-start.1 = ((bf16[32,2,384]{2,1,0:T(2,128)(2,1)}), bf16[32,2,384]{2,1,0:T(2,128)(2,1)S(1)}, u32[]{:S(2)}, u32[]{:S(2)}) async-start(bf16[32,2,384]{2,1,0:T(2,128)(2,1)} %reshape.163), calls=%async_computation.1 | async-start | bytes 98304 | tf_op jit(solution)/shard_map/all_to_all | solution.py:129
  32.1 1.8 scatter_custom_fusion.1
  34.9 5.1 %all-to-all-done.1 = bf16[32,2,384]{2,1,0:T(2,128)(2,1)S(1)} async-done(((bf16[32,2,384]{2,1,0:T(2,128)(2,1)}), bf16[32,2,384]{2,1,0:T(2,128)(2,1)S(1)}, u32[]{:S(2)}, u32[]{:S(2)}) %all-to-all-start.1) | async-done | bytes 49184 | tf_op jit(solution)/shard_map/all_to_all | solution.py:129
  39.9 5.0 all-to-all-start.2
  45.0 1.6 fusion.9
  46.7 30.2 %all-to-all-done.2 = bf16[32,12,768]{2,1,0:T(8,128)(2,1)S(1)} async-done(((bf16[32,12,768]{2,1,0:T(8,128)(2,1)}), bf16[32,12,768]{2,1,0:T(8,128)(2,1)S(1)}, u32[]{:S(2)}, u32[]{:S(2)}) %all-to-all-start.2) | async-done | bytes 589856 | tf_op jit(solution)/shard_map/all_to_all | solution.py:122
  76.9 3.4 stack.2
  80.2 4.7 all-to-all-start
  86.0 25.1 %all-gather.4.cloned.1.call-done = bf16[4096,768]{1,0:T(8,128)(2,1)} async-done(((bf16[128,768]{1,0:T(8,128)(2,1)}), bf16[4096,768]{1,0:T(8,128)(2,1)}) %all-gather.4.cloned.1.call-update) | async-done | bytes 6291472 | tf_op jit(solution)/shard_map/all_gather | solution.py:80
  111.2 33.8 %while.37 = (s32[]{:T(128)}, f32[8,512]{1,0:T(8,128)S(1)}, f32[8,512]{1,0:T(8,128)}, bf16[8,512,768]{2,1,0:T(8,128)(2,1)}, bf16[768,768]{1,0:T(8,128)(2,1)}, /*index=5*/f32[768]{0:T(1024)S(1)}, s32[]{:T(128)}, s32[]{:T(128)}) while((s32[]{:T(128)}, f32[8,512]{1,0:T(8,128)S(1)}, f32[8,512]{1,0:T(8,128)}, bf16[8,512,768]{2,1,0:T(8,128)(2,1)}, ...), condition=%wide.region_4.5_spmd, body=%wide.region_1.4_spmd.sunk | while | flops 605944832 | bytes 5129821 | solution.py:41
  111.2 2.4 fusion.37
  115.4 2.4 fusion.37
  118.2 1.3 dynamic_update_slice.10
  119.6 2.4 fusion.37
  123.9 2.4 fusion.37
  128.1 2.4 fusion.37
  130.9 1.3 dynamic_update_slice.10
  132.3 2.4 fusion.37
  135.1 1.3 dynamic_update_slice.10
  136.5 2.4 fusion.37
  139.4 1.3 dynamic_update_slice.10
  140.8 2.4 fusion.37
  145.6 104.2 %all-gather = f32[32,1,4096]{2,1,0:T(1,128)S(1)} all-gather(f32[1,1,4096]{2,1,0:T(1,128)S(1)} %reshape.146), channel_id=1, replica_groups=mesh['blk'=32,'dp'=8] {'blk'}, dimensions={0}, use_global_device_ids=true | all-gather | bytes 540672 | tf_op jit(solution)/shard_map/all_gather | solution.py:12
  250.6 36.3 %all-gather.1 = f32[32,1,4096]{2,1,0:T(1,128)S(1)} all-gather(f32[1,1,4096]{2,1,0:T(1,128)S(1)} %reshape.148), channel_id=1, replica_groups=mesh['blk'=32,'dp'=8] {'blk'}, dimensions={0}, use_global_device_ids=true | all-gather | bytes 540672 | tf_op jit(solution)/shard_map/all_gather | solution.py:12
  288.3 30.3 %while.38 = (s32[]{:T(128)}, f32[4096]{0:T(1024)S(1)}, f32[4096]{0:T(1024)S(1)}, f32[31,4096]{1,0:T(8,128)}, f32[31,4096]{1,0:T(8,128)S(1)}, /*index=5*/s32[]{:T(128)}) while((s32[]{:T(128)}, f32[4096]{0:T(1024)S(1)}, f32[4096]{0:T(1024)S(1)}, f32[31,4096]{1,0:T(8,128)}, f32[31,4096]{1,0:T(8,128)S(1)}, /*index=5*/s32[]{:T(128)}) %tuple.85), condition=%wide.region_6.7_spmd, body=%wide.region_5.6_spmd.sunk | while | flops 24578 | bytes 163913 | solution.py:15
  318.6 44.7 %while.39 = (s32[]{:T(128)}, f32[768,768]{1,0:T(8,128)S(1)}, f32[768]{0:T(1024)}, bf16[8,512,768]{2,1,0:T(8,128)(2,1)}, bf16[768,768]{1,0:T(8,128)(2,1)}, /*inde...) while((s32[]{:T(128)}, f32[768,768]{1,0:T(8,128)S(1)}, ...), condition=%wide.region_9.10_spmd.clone, body=%wide.region_7.9_spmd.clone.sunk | while | flops 1211892480 | bytes 9098412 | solution.py:65
  318.7 2.4 convert_reduce_fusion.3
  321.1 2.5 select_add_fusion.4
  324.3 2.4 convert_reduce_fusion.3
  326.7 2.5 select_add_fusion.4
  329.8 2.4 convert_reduce_fusion.3
  332.3 2.5 select_add_fusion.4
  335.4 2.4 convert_reduce_fusion.3
  337.9 2.5 select_add_fusion.4
  341.0 2.4 convert_reduce_fusion.3
  343.5 2.5 select_add_fusion.4
  346.6 2.4 convert_reduce_fusion.3
  349.0 2.5 select_add_fusion.4
  352.2 2.4 convert_reduce_fusion.3
  354.6 2.5 select_add_fusion.4
  357.7 2.4 convert_reduce_fusion.3
  360.2 2.5 select_add_fusion.4
  363.3 1.4 copy-done
  364.8 23.3 %all-reduce = (f32[768]{0:T(1024)S(1)}, f32[64]{0:T(128)S(1)}) all-reduce(f32[768]{0:T(1024)S(1)} %copy-done.4, f32[64]{0:T(128)S(1)} %convert_reduce_fusion.1), channel_id=1, replica_groups=mesh['blk'=32,'dp'=8] {'dp'}, use_global_device_ids=true, to_apply=%region_11.12 | all-reduce | flops 832 | bytes 6656 | tf_op jit(solution)/shard_map/psum | solution.py:145
  388.1 107.6 %all-reduce.4.cloned.1.call-done = (f32[768,768]{1,0:T(8,128)}, f32[64,768]{1,0:T(8,128)}) async-done(((f32[768,768]{1,0:T(8,128)}, f32[64,768]{1,0:T(8,128)}), (f32[768,768]{1,0:T(8,128)}, f32[64,768]{1,0:T(8,128)})) %all-reduce.4.cloned.1.call-update) | async-done | bytes 2555920 | tf_op jit(solution)/shard_map/psum | solution.py:145
  495.7 1.7 broadcast_divide_fusion
  497.4 3.7 fusion.11
  (181 shorter events, 54.9 us)
Async XLA Ops:
  7.2 104.0 %all-gather.4.cloned.1.call-start = ((), (), s32[]{:S(2)}) async-start(), calls=%async_computation.3 | async-start | bytes 6488064 | tf_op jit(solution)/shard_map/all_gather | solution.py:80
  22.6 17.3 %all-to-all-start.1 = ((bf16[32,2,384]{2,1,0:T(2,128)(2,1)}), bf16[32,2,384]{2,1,0:T(2,128)(2,1)S(1)}, u32[]{:S(2)}, u32[]{:S(2)}) async-start(bf16[32,2,384]{2,1,0:T(2,128)(2,1)} %reshape.163), calls=%async_computation.1 | async-start | bytes 98304 | tf_op jit(solution)/shard_map/all_to_all | solution.py:129
  32.1 44.8 %copy-start.1 = (bf16[128,768]{1,0:T(8,128)(2,1)S(1)}, bf16[128,768]{1,0:T(8,128)(2,1)}, u32[]{:S(2)}) copy-start(bf16[128,768]{1,0:T(8,128)(2,1)} %param.10) | copy-start | bytes 589828
  39.9 36.9 %all-to-all-start.2 = ((bf16[32,12,768]{2,1,0:T(8,128)(2,1)}), bf16[32,12,768]{2,1,0:T(8,128)(2,1)S(1)}, u32[]{:S(2)}, u32[]{:S(2)}) async-start(bf16[32,12,768]{2,1,0:T(8,128)(2,1)} %reshape.129), calls=%async_computation.2 | async-start | bytes 1572864 | tf_op jit(solution)/shard_map/all_to_all | solution.py:122
  80.2 238.4 %all-to-all-start = ((bf16[32,128,768]{2,1,0:T(8,128)(2,1)}), bf16[32,128,768]{2,1,0:T(8,128)(2,1)}, u32[]{:S(2)}, u32[]{:S(2)}) async-start(bf16[32,128,768]{2,1,0:T(8,128)(2,1)} %stack.2), calls=%async_computation | async-start | bytes 12582912 | tf_op jit(solution)/shard_map/all_to_all | solution.py:93
  85.0 410.8 %all-reduce.4.cloned.1.call-start = ((), (), s32[]{:S(2)}) async-start(), calls=%async_computation.4 | async-start | bytes 5111808 | tf_op jit(solution)/shard_map/psum | solution.py:145
  145.0 0.6 copy-start.5
  321.1 2.5 copy-start.2
  323.6 0.6 copy-start.3
  326.7 2.5 copy-start.2
  329.2 0.6 copy-start.3
  332.3 2.5 copy-start.2
  334.8 0.6 copy-start.3
  337.9 2.5 copy-start.2
  340.4 0.6 copy-start.3
  343.5 2.5 copy-start.2
  346.0 0.6 copy-start.3
  349.0 2.5 copy-start.2
  351.6 0.6 copy-start.3
  354.6 2.5 copy-start.2
  357.1 0.6 copy-start.3
  360.2 2.5 copy-start.2
  362.7 0.6 copy-start.3
  363.3 1.4 copy-start
  363.3 1.5 copy-start.4
Sparse Core Ops, SparseCore 0:
  9.9 101.2 all-gather.3
  364.9 130.8 all-reduce.3
